TPU v7x, 32 devices: a whole 2x2x4 slice. The times are simulated.
32 devices in a mesh: grp: 2 (over y), slab: 4 (over z), mem: 2 (over x), sub: 2 (over core).
Axes of the slice: x: 2, y: 2, z: 4, core: 2. Of those that a mesh axis runs over, the one named last changes fastest.
Arguments:
- state: bfloat16 [256, 32768], P('mem', ('grp', 'slab', 'sub')), parts along dimension 1, may hold values from -6 to 6
- centers: int32 [512], P('grp'), parts along dimension 0, may hold values from 0 to 16383, as said below
- half_width: int32 [512], P('grp'), parts along dimension 0, may hold values from 4 to 71
- radius: int32 [512], P('grp'), parts along dimension 0, may hold values from 2048 to 8192
- order: int32 [512], P('grp'), parts along dimension 0, may hold values from 0 to 255, each once
- obs_var: float32 [512], P('grp'), parts along dimension 0, may hold values from 0.1 to 1
Outputs:
- analysis: bfloat16 [256, 32768], P('mem', ('grp', 'slab', 'sub')), parts along dimension 1
There are 2 independent parts, one for each index of `grp`. A program takes and returns all parts, laid end to end along the dimension named above; each array names one. Nothing has to cross between parts.
Inputs may be any that keep to these rules, and one draw needn't show every extreme that they name: order holds every observation number once. Observations 4 k to 4 k + 3 have centers within 6 rows of a common site row, which the first of them sits on; centers are clipped to the grid.
All inputs are finite; a program needn't handle non-finite values.
Results may differ from a plain program's by a relative error of at most 0.0049.
Values may be sent and summed in bfloat16 or wider, within the bound.
A program may use at most 64 MiB of HBM per device.

v0:
```python
import math
import jax
import jax.numpy as jnp
from jax import lax
from jax.sharding import PartitionSpec as P

M = 256
P_SIZE = 128
BATCHES = 2
floor_level = math.exp(-2.0)


def geometry(first_row, row_count, center_rows, half_rows, radius_rows):
    rows_all = first_row + lax.iota(jnp.int32, row_count)
    distance = (rows_all[None, :] - center_rows[:, None]).astype(jnp.float32)
    half_f = half_rows.astype(jnp.float32)[:, None]
    footprint = (
        jnp.maximum(jnp.exp(-2.0 * distance * distance / (half_f * half_f)) - floor_level, 0.0)
        / jnp.sqrt(half_f)
    ).astype(jnp.bfloat16)
    taper_rows = jnp.square(
        jnp.maximum(1.0 - jnp.abs(distance) / radius_rows.astype(jnp.float32)[:, None], 0.0)
    )
    return (footprint, taper_rows)


def gain_terms(projected, variance):
    high = lax.Precision.HIGHEST
    covariance = jnp.dot(
        projected.T, projected, precision=high, preferred_element_type=jnp.float32
    ) / (M - 1) + jnp.diag(variance)
    factor = jnp.linalg.cholesky(covariance)
    identity = jnp.eye(P_SIZE, dtype=jnp.float32)
    inner_inv = lax.linalg.triangular_solve(
        factor + jnp.diag(jnp.sqrt(variance)), identity, left_side=True, lower=True
    )
    gain_mat = lax.linalg.triangular_solve(
        factor, inner_inv, left_side=True, lower=True, transpose_a=True
    )
    weights = jnp.dot(
        projected, gain_mat.T, precision=high, preferred_element_type=jnp.float32
    ).astype(jnp.bfloat16)
    return (weights, projected.astype(jnp.bfloat16))


def project_rows(ensemble, footprint):
    return lax.dot_general(
        ensemble, footprint, (((1,), (1,)), ((), ())), preferred_element_type=jnp.float32
    )


def cross_rows(projected_b, ensemble):
    return lax.dot_general(
        projected_b, ensemble, (((0,), (0,)), ((), ())), preferred_element_type=jnp.float32
    )


def on_device(state, centers, half_width, radius, order, obs_var):
    own_count, rows_here = state.shape
    row_base = lax.axis_index(("slab", "sub")) * rows_here
    centers_all = centers[order]
    half_all = half_width[order]
    radius_all = radius[order]
    variance_all = obs_var[order]
    ensemble = state
    offset = lax.axis_index("mem") * own_count
    for batch in range(BATCHES):
        lo_obs = batch * P_SIZE
        footprint, taper_rows = geometry(
            row_base,
            rows_here,
            centers_all[lo_obs : lo_obs + P_SIZE],
            half_all[lo_obs : lo_obs + P_SIZE],
            radius_all[lo_obs : lo_obs + P_SIZE],
        )
        partial_value = project_rows(ensemble, footprint)
        summed_own = lax.psum(partial_value, ("slab", "sub"))
        projected = lax.all_gather(summed_own, "mem", axis=0, tiled=True)
        weights, projected_b = gain_terms(projected, variance_all[lo_obs : lo_obs + P_SIZE])
        cross_cov = cross_rows(projected_b, lax.all_gather(ensemble, "mem", axis=0, tiled=True))
        tapered = (taper_rows * cross_cov / (M - 1)).astype(jnp.bfloat16)
        weights_own = lax.dynamic_slice_in_dim(weights, offset, own_count, 0)
        ensemble = (
            ensemble.astype(jnp.float32)
            - jnp.dot(weights_own, tapered, preferred_element_type=jnp.float32)
        ).astype(jnp.bfloat16)
    return ensemble


def solution(mesh):
    placed = (P("mem", ("grp", "slab", "sub")), P("grp"), P("grp"), P("grp"), P("grp"), P("grp"))
    return jax.shard_map(
        on_device,
        mesh=mesh,
        in_specs=placed,
        out_specs=P("mem", ("grp", "slab", "sub")),
        check_vma=False,
    )
```

profile of v0, /device:TPU:0, one launch (start us, length us, event | category | flops | bytes accessed | tf_op | source)
XLA Modules:
  0.0 215.7 jit_solution(16010699349236108994)
XLA Ops:
  7.4 0.0 copy-start
  7.4 0.0 all-reduce.3.cloned.1.call-start
  7.4 0.0 copy-start.8
  7.4 0.7 copy-done.8
  8.1 0.0 copy-done
  8.1 1.9 gather_fusion.1
  10.0 0.0 copy-start.1
  10.1 0.7 copy-done.1
  10.7 0.0 copy-start.4
  10.7 1.9 gather_fusion
  12.7 0.0 copy-done.4
  12.7 1.2 convolution_bitcast_fusion
  13.9 0.0 all-reduce.3.cloned.1.call-update
  13.9 0.0 all-gather.3.cloned.1.call-start
  14.0 0.5 all-gather.3.cloned.1.call-update
  14.5 0.0 copy-start.2
  14.5 0.0 all-reduce.5.cloned.1.call-start
  14.6 0.6 copy-done.2
  15.2 1.9 gather_fusion.2
  17.2 0.0 copy-start.3
  17.2 0.7 copy-done.3
  17.9 1.9 gather_fusion.3
  19.8 50.6 %all-reduce.3.cloned.1.call-done = f32[128,128]{0,1:T(8,128)} async-done(((f32[128,128]{0,1:T(8,128)}), f32[128,128]{0,1:T(8,128)}) %all-reduce.3.cloned.1.call-update) | async-done | bytes 65552 | tf_op jit(solution)/shard_map/psum | solution.py:77
  70.4 5.3 %all_gather.12 = f32[256,128]{0,1:T(8,128)S(1)} all-gather(f32[128,128]{0,1:T(8,128)} %all-reduce.3.cloned.1.call-done), channel_id=1, replica_groups=mesh['grp'=2,'slab'=4,'mem'=2,'sub'=2] {'mem'}, dimensions={0}, use_global_device_ids=true | all-gather | bytes 196608 | tf_op jit(solution)/shard_map/all_gather | solution.py:78
  75.7 0.3 fusion.6
  76.0 0.1 copy.11
  76.1 0.0 copy-start.5
  76.1 0.1 copy.12
  76.2 11.7 %cholesky.44 = f32[128,128]{1,0:T(8,128)S(1)} custom-call(f32[128,128]{1,0:T(8,128)S(1)} %copy.12), custom_call_target="Cholesky" | custom-call | tf_op jit(solution)/shard_map/jit(cholesky)/cholesky | solution.py:32
  88.0 0.6 compare_reduce_fusion.1
  88.6 0.7 select_bitcast_fusion.2
  89.4 9.8 %custom-call.10 = f32[1,128,128]{1,2,0:T(8,128)S(1)} custom-call(f32[1,128,128]{2,1,0:T(8,128)S(1)} %get-tuple-element.11), custom_call_target="InvertDiagBlocksLowerTriangular" | custom-call | tf_op jit(solution)/shard_map/triangular_solve/custom-call.0 | solution.py:34
  99.2 9.8 %custom-call.11 = f32[1,128,128]{1,2,0:T(8,128)S(1)} custom-call(f32[1,128,128]{2,1,0:T(8,128)S(1)} %get-tuple-element.10), custom_call_target="InvertDiagBlocksLowerTriangular" | custom-call | tf_op jit(solution)/shard_map/triangular_solve/custom-call.2 | solution.py:37
  109.0 0.3 fusion.65
  109.3 0.2 fusion.72
  109.5 0.4 fusion.103
  109.9 0.0 all-gather.3.cloned.1.call-done
  109.9 0.0 copy-done.5
  109.9 2.0 fusion.4
  111.9 0.0 copy-start.6
  111.9 1.3 fusion.35
  113.2 0.0 copy-done.6
  113.2 0.0 all-reduce.5.cloned.1.call-update
  113.2 0.0 all-gather.5.cloned.1.call-start
  113.3 0.5 all-gather.5.cloned.1.call-update
  113.8 52.2 %all-reduce.5.cloned.1.call-done = f32[128,128]{1,0:T(8,128)} async-done(((f32[128,128]{1,0:T(8,128)}), f32[128,128]{1,0:T(8,128)}) %all-reduce.5.cloned.1.call-update) | async-done | bytes 65552 | tf_op jit(solution)/shard_map/psum | solution.py:77
  166.0 5.4 %all_gather.14 = f32[256,128]{1,0:T(8,128)S(1)} all-gather(f32[128,128]{1,0:T(8,128)} %all-reduce.5.cloned.1.call-done), channel_id=1, replica_groups=mesh['grp'=2,'slab'=4,'mem'=2,'sub'=2] {'mem'}, dimensions={0}, use_global_device_ids=true | all-gather | bytes 196608 | tf_op jit(solution)/shard_map/all_gather | solution.py:78
  171.3 0.4 fusion.7
  171.7 0.1 copy.13
  171.8 0.0 copy-start.7
  171.8 0.1 copy.14
  171.9 11.7 %cholesky.55 = f32[128,128]{1,0:T(8,128)S(1)} custom-call(f32[128,128]{1,0:T(8,128)S(1)} %copy.14), custom_call_target="Cholesky" | custom-call | tf_op jit(solution)/shard_map/jit(cholesky)/cholesky | solution.py:32
  183.7 0.7 compare_reduce_fusion
  184.4 0.7 select_bitcast_fusion
  185.1 9.8 %custom-call.12 = f32[1,128,128]{1,2,0:T(8,128)S(1)} custom-call(f32[1,128,128]{2,1,0:T(8,128)S(1)} %get-tuple-element.8), custom_call_target="InvertDiagBlocksLowerTriangular" | custom-call | tf_op jit(solution)/shard_map/triangular_solve/custom-call.0 | solution.py:34
  194.9 9.8 %custom-call.13 = f32[1,128,128]{1,2,0:T(8,128)S(1)} custom-call(f32[1,128,128]{2,1,0:T(8,128)S(1)} %get-tuple-element.6), custom_call_target="InvertDiagBlocksLowerTriangular" | custom-call | tf_op jit(solution)/shard_map/triangular_solve/custom-call.2 | solution.py:37
  204.7 0.3 fusion.63
  205.0 0.2 fusion.68
  205.2 0.3 fusion.104
  205.5 0.0 all-gather.5.cloned.1.call-done
  205.5 0.0 copy-done.7
  205.5 2.8 %fusion.5 = bf16[128,2048]{1,0:T(8,128)(2,1)} fusion(bf16[256,2048]{1,0:T(8,128)(2,1)} %all-gather.5.cloned.1.call-done, bf16[128,2048]{1,0:T(8,128)(2,1)S(1)} %copy-done.7, f32[128]{0:T(128)S(1)} %get-tuple-element.22, s32[128]{0:T(128)S(1)} %get-tuple-element.20, s32[2048]{0:T(1024)S(1)} %iota_add_fusion, f32[256,128]{1,0:T(8,128)S(1)} %all_gather.14, ...), kind=kOutput, calls=%fused_computation.13 | convolution fusion | flops 204767232 | bytes 2270212 | tf_op jit(solution)/shard_map/dot_general | solution.py:85
  (11 shorter events, 0.1 us)
Async XLA Ops:
  7.4 0.7 copy-start
  7.4 63.0 %all-reduce.3.cloned.1.call-start = ((), (), s32[]{:S(2)}) async-start(), calls=%async_computation | async-start | bytes 131072 | tf_op jit(solution)/shard_map/psum | solution.py:77
  7.4 0.7 copy-start.8
  10.0 0.7 copy-start.1
  10.7 2.0 copy-start.4
  13.9 96.0 %all-gather.3.cloned.1.call-start = ((), (), s32[]{:S(2)}) async-start(), calls=%async_computation.1 | async-start | bytes 1572864 | tf_op jit(solution)/shard_map/all_gather | solution.py:80
  14.5 0.7 copy-start.2
  14.5 151.4 %all-reduce.5.cloned.1.call-start = ((), (), s32[]{:S(2)}) async-start(), calls=%async_computation.2 | async-start | bytes 131072 | tf_op jit(solution)/shard_map/psum | solution.py:77
  17.2 0.7 copy-start.3
  76.1 33.8 %copy-start.5 = (bf16[128,2048]{1,0:T(8,128)(2,1)S(1)}, bf16[128,2048]{1,0:T(8,128)(2,1)}, u32[]{:S(2)}) copy-start(bf16[128,2048]{1,0:T(8,128)(2,1)} %param.11) | copy-start | bytes 1572868
  111.9 1.3 copy-start.6
  113.2 92.3 %all-gather.5.cloned.1.call-start = ((), (), s32[]{:S(2)}) async-start(), calls=%async_computation.3 | async-start | bytes 1572864 | tf_op jit(solution)/shard_map/all_gather | solution.py:80
  171.8 33.7 %copy-start.7 = (bf16[128,2048]{1,0:T(8,128)(2,1)S(1)}, bf16[128,2048]{1,0:T(8,128)(2,1)}, u32[]{:S(2)}) copy-start(bf16[128,2048]{1,0:T(8,128)(2,1)} %copy-done.6) | copy-start | bytes 1572868
Sparse Core Ops, SparseCore 0:
  14.1 56.3 all-reduce.2
  113.3 52.5 all-reduce.4
Sparse Core Ops, SparseCore 1:
  16.0 23.9 all-gather.2
  115.3 20.2 all-gather.4
where the time goes:
time: 216 us
  waiting for transfers between devices  104 us (48%)
  other arithmetic  65.5 us (30%)
  between operations  15.2 us (7%)
  local copies, waits for them, and re-layouts  10.8 us (5%)
  blocking collectives  10.7 us (5%)
  matrix products  9.54 us (4%)
    psum x2, waiting for transfers between devices, on_device(): summed_own = lax.psum(partial_value, ('slab', 'sub'))  103 us
    another operation x6, other arithmetic, gain_terms(): factor = jnp.linalg.cholesky(covariance)  24.8 us
    another operation x4, other arithmetic, gain_terms(): lax.linalg.triangular_solve(factor, inner_inv, left_side=True, lower=True...  21 us
    another operation x2, other arithmetic, gain_terms(): lax.linalg.triangular_solve(factor + jnp.diag(jnp.sqrt(variance)), identi...  19.6 us
    all_gather x2, blocking collectives, on_device(): projected = lax.all_gather(summed_own, 'mem', axis=0, tiled=True)  10.7 us
    dot_general x2, matrix products, on_device(): jnp.dot(weights_own, tapered, preferred_element_type=jnp.float32)  4.76 us
  transfers between devices with their start and end apart: 4, of which 2 were waited for; matrix products, arithmetic and copies ran while one was open for 33% of the time, Pallas kernels for 0%

commit v1 on v0

--- a/solution.py
+++ b/solution.py
@@ -74,7 +74,7 @@
             radius_all[lo_obs : lo_obs + P_SIZE],
         )
         partial_value = project_rows(ensemble, footprint)
-        summed_own = lax.psum(partial_value, ("slab", "sub"))
+        summed_own = jnp.sum(lax.all_gather(partial_value, ("slab", "sub")), axis=0)
         projected = lax.all_gather(summed_own, "mem", axis=0, tiled=True)
         weights, projected_b = gain_terms(projected, variance_all[lo_obs : lo_obs + P_SIZE])
         cross_cov = cross_rows(projected_b, lax.all_gather(ensemble, "mem", axis=0, tiled=True))

time: 216 us -> 144 us (0.67)
  waiting for transfers between devices: 104 us -> 0.77 us
  blocking collectives: 10.7 us -> 43.6 us
    psum x2 -> x0, waiting for transfers between devices: 103 us -> none  [on_device(): summed_own = lax.psum(partial_value, ('slab', 'sub'))]
    all_gather x0 -> x2, blocking collectives: none -> 31.4 us  [on_device(): summed_own = jnp.sum(lax.all_gather(partial_value, ('slab', 'sub')), axis=0)]
  transfers between devices with their start and end apart: 4 -> 2, of which waited for: 2 -> 0; matrix products, arithmetic and copies ran while one was open for 33% -> 54% of each run, Pallas kernels for 0% -> 0%
where the time goes in v1:
time: 144 us
  other arithmetic  65.7 us (46%)
  blocking collectives  43.6 us (30%)
  between operations  13.7 us (10%)
  local copies, waits for them, and re-layouts  11.3 us (8%)
  matrix products  9.06 us (6%)
    all_gather x2, blocking collectives, on_device(): summed_own = jnp.sum(lax.all_gather(partial_value, ('slab', 'sub')), axis=0)  31.4 us
    another operation x6, other arithmetic, gain_terms(): factor = jnp.linalg.cholesky(covariance)  24.8 us
    another operation x4, other arithmetic, gain_terms(): lax.linalg.triangular_solve(factor, inner_inv, left_side=True, lower=True...  21.1 us
    another operation x2, other arithmetic, gain_terms(): lax.linalg.triangular_solve(factor + jnp.diag(jnp.sqrt(variance)), identi...  19.6 us
    all_gather x2, blocking collectives, on_device(): projected = lax.all_gather(summed_own, 'mem', axis=0, tiled=True)  12.1 us
    dot_general x2, matrix products, on_device(): jnp.dot(weights_own, tapered, preferred_element_type=jnp.float32)  5.54 us
    unnamed x15, local copies, waits for them, and re-layouts  3.12 us
  transfers between devices with their start and end apart: 2, of which 0 were waited for; matrix products, arithmetic and copies ran while one was open for 54% of the time, Pallas kernels for 0%

profile of v1, /device:TPU:0, one launch (start us, length us, event | category | flops | bytes accessed | tf_op | source)
XLA Modules:
  0.0 144.1 jit_solution(18310845273632824136)
XLA Ops:
  6.5 0.0 copy-start
  6.5 0.0 all-gather.5.cloned.1.call-start
  6.5 0.7 all-gather.5.cloned.1.call-update
  7.3 0.0 all-gather.7.cloned.1.call-start
  7.3 0.0 copy-start.6
  7.3 0.7 copy-done.6
  8.0 0.0 copy-done
  8.0 1.9 %gather_fusion.1 = s32[256]{0:T(256)S(1)} fusion(s32[256]{0:T(256)S(1)} %copy-done, s32[1024]{0:T(1024)S(1)} %pad_clamp_fusion), kind=kCustom, calls=%fused_computation.1 | custom fusion | bytes 3072 | tf_op jit(solution)/shard_map/gather | solution.py:62
  10.0 0.0 copy-start.1
  10.0 0.7 copy-done.1
  10.6 0.0 copy-start.4
  10.7 1.9 %gather_fusion = s32[256]{0:T(256)S(1)} fusion(s32[256]{0:T(256)S(1)} %copy-done.1, s32[1024]{0:T(1024)S(1)} %pad_clamp_fusion), kind=kCustom, calls=%fused_computation | custom fusion | bytes 3072 | tf_op jit(solution)/shard_map/gather | solution.py:61
  12.6 0.0 copy-done.4
  12.6 0.6 convolution_bitcast_fusion
  13.2 16.5 %all-gather = f32[1024,128]{0,1:T(8,128)S(1)} all-gather(f32[128,128]{0,1:T(8,128)S(1)} %convolution_bitcast_fusion), channel_id=2, replica_groups=mesh['grp'=2,'slab'=4,'mem'=2,'sub'=2] {'slab','sub'}, dimensions={0}, use_global_device_ids=true | all-gather | bytes 589824 | tf_op jit(solution)/shard_map/all_gather | solution.py:77
  29.7 0.1 copy.19
  29.8 0.1 bitcast_reduce_fusion
  29.9 0.0 copy-start.2
  29.9 5.2 %all_gather.26 = f32[256,128]{0,1:T(8,128)S(1)} all-gather(f32[128,128]{0,1:T(8,128)S(1)} %bitcast_reduce_fusion), channel_id=1, replica_groups=mesh['grp'=2,'slab'=4,'mem'=2,'sub'=2] {'mem'}, dimensions={0}, use_global_device_ids=true | all-gather | bytes 196608 | tf_op jit(solution)/shard_map/all_gather | solution.py:78
  35.1 0.0 copy-done.2
  35.1 1.9 %gather_fusion.2 = f32[256]{0:T(256)S(1)} fusion(f32[256]{0:T(256)S(1)} %copy-done.2, s32[1024]{0:T(1024)S(1)} %pad_clamp_fusion), kind=kCustom, calls=%fused_computation.2 | custom fusion | bytes 3072 | tf_op jit(solution)/shard_map/gather | solution.py:64
  37.1 0.3 fusion.6
  37.4 0.1 copy.15
  37.5 0.1 copy.16
  37.6 11.7 %cholesky.44 = f32[128,128]{1,0:T(8,128)S(1)} custom-call(f32[128,128]{1,0:T(8,128)S(1)} %copy.16), custom_call_target="Cholesky" | custom-call | tf_op jit(solution)/shard_map/jit(cholesky)/cholesky | solution.py:32
  49.4 0.6 compare_reduce_fusion.1
  50.0 0.7 select_bitcast_fusion.2
  50.7 9.8 %custom-call.10 = f32[1,128,128]{1,2,0:T(8,128)S(1)} custom-call(f32[1,128,128]{2,1,0:T(8,128)S(1)} %get-tuple-element.11), custom_call_target="InvertDiagBlocksLowerTriangular" | custom-call | tf_op jit(solution)/shard_map/triangular_solve/custom-call.0 | solution.py:34
  60.5 9.8 %custom-call.11 = f32[1,128,128]{1,2,0:T(8,128)S(1)} custom-call(f32[1,128,128]{2,1,0:T(8,128)S(1)} %get-tuple-element.10), custom_call_target="InvertDiagBlocksLowerTriangular" | custom-call | tf_op jit(solution)/shard_map/triangular_solve/custom-call.2 | solution.py:37
  70.4 0.0 copy-start.3
  70.4 0.7 copy-done.3
  71.1 1.9 %gather_fusion.3 = s32[256]{0:T(256)S(1)} fusion(s32[256]{0:T(256)S(1)} %copy-done.3, s32[1024]{0:T(1024)S(1)} %pad_clamp_fusion), kind=kCustom, calls=%fused_computation.3 | custom fusion | bytes 3072 | tf_op jit(solution)/shard_map/gather | solution.py:63
  73.0 0.3 fusion.65
  73.3 0.2 fusion.72
  73.5 0.4 fusion.103
  73.9 0.0 all-gather.5.cloned.1.call-done
  73.9 2.8 %fusion.4 = bf16[128,2048]{1,0:T(8,128)(2,1)} fusion(bf16[256,2048]{1,0:T(8,128)(2,1)} %all-gather.5.cloned.1.call-done, bf16[128,2048]{1,0:T(8,128)(2,1)S(1)} %copy-done.4, f32[128]{0:T(128)S(1)} %get-tuple-element.23, s32[128]{0:T(128)S(1)} %get-tuple-element.21, s32[2048]{0:T(1024)S(1)} %iota_add_fusion, f32[256,128]{0,1:T(8,128)S(1)} %all_gather.26, ...), kind=kOutput, calls=%fused_computation.12 | convolution fusion | flops 204767232 | bytes 2270212 | tf_op jit(solution)/shard_map/dot_general | solution.py:85
  76.7 0.0 copy-start.5
  76.7 0.0 all-gather.7.cloned.1.call-update
  76.7 1.0 copy-done.5
  77.7 0.6 fusion.35
  78.4 14.9 %all-gather.1 = f32[1024,128]{1,0:T(8,128)S(1)} all-gather(f32[128,128]{1,0:T(8,128)S(1)} %fusion.35), channel_id=3, replica_groups=mesh['grp'=2,'slab'=4,'mem'=2,'sub'=2] {'slab','sub'}, dimensions={0}, use_global_device_ids=true | all-gather | bytes 589824 | tf_op jit(solution)/shard_map/all_gather | solution.py:77
  93.3 6.9 %all_gather.30 = f32[256,128]{1,0:T(8,128)S(1)} all-gather(f32[128,128]{1,0:T(8,128)S(1)} %reduce_sum.19), channel_id=1, replica_groups=mesh['grp'=2,'slab'=4,'mem'=2,'sub'=2] {'mem'}, dimensions={0}, use_global_device_ids=true | all-gather | bytes 196608 | tf_op jit(solution)/shard_map/all_gather | solution.py:78
  100.3 0.4 fusion.7
  100.7 0.1 copy.17
  100.8 0.1 copy.18
  100.9 11.7 %cholesky.55 = f32[128,128]{1,0:T(8,128)S(1)} custom-call(f32[128,128]{1,0:T(8,128)S(1)} %copy.18), custom_call_target="Cholesky" | custom-call | tf_op jit(solution)/shard_map/jit(cholesky)/cholesky | solution.py:32
  112.6 0.7 compare_reduce_fusion
  113.3 0.7 select_bitcast_fusion
  114.0 9.8 %custom-call.12 = f32[1,128,128]{1,2,0:T(8,128)S(1)} custom-call(f32[1,128,128]{2,1,0:T(8,128)S(1)} %get-tuple-element.8), custom_call_target="InvertDiagBlocksLowerTriangular" | custom-call | tf_op jit(solution)/shard_map/triangular_solve/custom-call.0 | solution.py:34
  123.8 9.8 %custom-call.13 = f32[1,128,128]{1,2,0:T(8,128)S(1)} custom-call(f32[1,128,128]{2,1,0:T(8,128)S(1)} %get-tuple-element.6), custom_call_target="InvertDiagBlocksLowerTriangular" | custom-call | tf_op jit(solution)/shard_map/triangular_solve/custom-call.2 | solution.py:37
  133.7 0.3 fusion.63
  133.9 0.2 fusion.68
  134.2 0.3 fusion.104
  134.4 0.0 all-gather.7.cloned.1.call-done
  134.5 2.8 %fusion.5 = bf16[128,2048]{1,0:T(8,128)(2,1)} fusion(bf16[256,2048]{1,0:T(8,128)(2,1)} %all-gather.7.cloned.1.call-done, bf16[128,2048]{1,0:T(8,128)(2,1)S(1)} %copy-done.5, f32[128]{0:T(128)S(1)} %get-tuple-element.22, s32[128]{0:T(128)S(1)} %get-tuple-element.20, s32[2048]{0:T(1024)S(1)} %iota_add_fusion, f32[256,128]{1,0:T(8,128)S(1)} %all_gather.30, ...), kind=kOutput, calls=%fused_computation.13 | convolution fusion | flops 204767232 | bytes 2270212 | tf_op jit(solution)/shard_map/dot_general | solution.py:85
  (12 shorter events, 0.2 us)
Async XLA Ops:
  6.5 1.5 %copy-start = (s32[256]{0:T(256)S(1)}, s32[256]{0:T(256)}, u32[]{:S(2)}) copy-start(s32[256]{0:T(256)} %param.13) | copy-start | bytes 3076
  6.5 67.4 %all-gather.5.cloned.1.call-start = ((), (), s32[]{:S(2)}) async-start(), calls=%async_computation | async-start | bytes 1572864 | tf_op jit(solution)/shard_map/all_gather | solution.py:80
  7.3 127.2 %all-gather.7.cloned.1.call-start = ((), (), s32[]{:S(2)}) async-start(), calls=%async_computation.1 | async-start | bytes 1572864 | tf_op jit(solution)/shard_map/all_gather | solution.py:80
  7.3 0.7 copy-start.6
  10.0 0.7 copy-start.1
  10.6 2.0 %copy-start.4 = (bf16[128,2048]{1,0:T(8,128)(2,1)S(1)}, bf16[128,2048]{1,0:T(8,128)(2,1)}, u32[]{:S(2)}) copy-start(bf16[128,2048]{1,0:T(8,128)(2,1)} %param.11) | copy-start | bytes 1572868
  29.9 5.2 %copy-start.2 = (f32[256]{0:T(256)S(1)}, f32[256]{0:T(256)}, u32[]{:S(2)}) copy-start(f32[256]{0:T(256)} %param.16) | copy-start | bytes 3076
  70.4 0.7 copy-start.3
  76.7 1.0 copy-start.5
Sparse Core Ops, SparseCore 0:
  8.9 23.9 all-gather.4
  76.8 23.8 all-gather.6
